TPU v7x, 128 devices: a whole 4x4x4 slice. The times are simulated.
128 devices in a mesh: grp: 16 (over x, y), blk: 8 (over z, core).
Axes of the slice: x: 4, y: 4, z: 4, core: 2. Of those that a mesh axis runs over, the one named last changes fastest.
Arguments:
- embeddings: bfloat16 [65536, 768], P(('grp', 'blk'))
- assign: int32 [65536], P(('grp', 'blk')), may hold values from 0 to 127, as said below
- owner: int32 [128], replicated, may hold values from 0 to 15, as said below
- send_count: int32 [128, 16], P(('grp', 'blk')), may hold values from 0 to 64, as said below
- send_index: int32 [128, 16, 64], P(('grp', 'blk')), may hold values from 0 to 511, as said below
Outputs:
- max_sim: float32 [65536], P(('grp', 'blk'))
- centroid_cos: float32 [65536], P(('grp', 'blk'))
Inputs may be any that keep to these rules, and one draw needn't show every extreme that they name: `owner`: every group owns the same number of clusters. `assign`: every document's cluster is owned by the group in whose list of its device the document stands; a device may send many documents of one cluster. `send_count`: A device's counts sum to 512; a count may be anything from 0 to 64, and at least one group receives exactly 64 documents from every device. `send_index`: the used slots of a device's lists hold each of its documents exactly once; unused slots hold 0.
All inputs are finite; a program needn't handle non-finite values.
Results may differ from a plain program's by a relative error of at most 0.00085.
Values may be sent and summed in bfloat16 or wider, within the bound.
A program may use at most 64 MiB of HBM per device.

v0:
```python
import functools

import jax
import jax.numpy as jnp
from jax import lax
from jax.experimental import pallas as pl
from jax.experimental.pallas import tpu as pltpu
from jax.sharding import PartitionSpec as P

EPSILON = 1e-06
F32 = jnp.float32
BF16 = jnp.bfloat16

CHIPS = 64
ROWS = 512
WIDTH = 768
CLUSTERS = 128
GROUPS = 16
CAP = 64
BASE = 16
HALF = WIDTH // 2
LINES = 16
DEPTH = 4
POOL = 8
PARTS = ((0, 40, 400), (40, 32, 256))
TOTAL = 72
HELD = 656
STARTS = (0, 400)
LAST = len(PARTS) - 1
NONE = 1e30


def normalize(values):
    widened = values.astype(F32)
    return widened * lax.rsqrt(jnp.sum(widened * widened, axis=1, keepdims=True) + EPSILON)


def general(embeddings, assign, owner, send_count, send_index):
    rows_local = embeddings.shape[0]
    feature_width = embeddings.shape[1]
    groups = lax.axis_size("grp")
    clusters = owner.shape[0]
    capacity = send_index.shape[2]
    slot_total = groups * capacity
    unit_rows = normalize(embeddings)
    unit_low = unit_rows.astype(BF16)
    counts = send_count[0]
    listed = send_index[0]
    live_slot = jnp.arange(capacity, dtype=jnp.int32)[None, :] < counts[:, None]
    listed_cluster = assign[listed]
    owned_here = owner[listed_cluster] == jnp.arange(groups, dtype=jnp.int32)[:, None]
    kept_slot = live_slot & owned_here
    out_cluster = jnp.where(kept_slot, listed_cluster, -1)
    out_tag = jnp.where(kept_slot, lax.axis_index(("grp", "blk")) * rows_local + listed, -1)
    out_vector = unit_low[listed.reshape(-1)].reshape(groups, capacity, feature_width)
    got_vector, got_cluster, got_tag = (
        lax.all_to_all(out_vector, "grp", split_axis=0, concat_axis=0, tiled=True),
        lax.all_to_all(out_cluster, "grp", split_axis=0, concat_axis=0, tiled=True),
        lax.all_to_all(out_tag, "grp", split_axis=0, concat_axis=0, tiled=True),
    )
    own_vector = got_vector.reshape(slot_total, feature_width)
    own_cluster = got_cluster.reshape(slot_total)
    own_tag = got_tag.reshape(slot_total)

    def tile_best(current, shard_piece):
        other_vector, other_cluster, other_tag = shard_piece
        scores = jnp.einsum("id,jd->ij", own_vector, other_vector, preferred_element_type=F32)
        matched = (
            (own_cluster[:, None] == other_cluster[None, :])
            & (other_cluster[None, :] >= 0)
            & (own_tag[:, None] != other_tag[None, :])
        )
        return jnp.maximum(current, jnp.max(jnp.where(matched, scores, -1.0), axis=1))

    other_vector = lax.all_gather(own_vector, "blk", axis=0, tiled=True)
    other_cluster = lax.all_gather(own_cluster, "blk", axis=0, tiled=True)
    other_tag = lax.all_gather(own_tag, "blk", axis=0, tiled=True)
    length = other_vector.shape[0]
    number = length // slot_total
    stacked = (
        other_vector.reshape(number, slot_total, feature_width),
        other_cluster.reshape(number, slot_total),
        other_tag.reshape(number, slot_total),
    )

    def scan_step(carry, single):
        return (tile_best(carry, single), None)

    result, unused = lax.scan(scan_step, jnp.full((slot_total,), -1.0, F32), stacked)
    target = jnp.where(live_slot, listed, rows_local).reshape(-1)
    partial_sum = jax.ops.segment_sum(unit_rows, assign, num_segments=clusters)
    centre = normalize(lax.psum(partial_sum, ("grp", "blk")))
    nearness = jnp.sum(unit_low.astype(F32) * centre[assign], axis=1)
    returned = lax.all_to_all(
        result.reshape(groups, capacity), "grp", split_axis=0, concat_axis=0, tiled=True
    )
    has_entry = (
        jnp.zeros((rows_local,), jnp.int32)
        .at[target]
        .max(kept_slot.astype(jnp.int32).reshape(-1), mode="drop")
    )
    centroid_cos = jnp.where(has_entry > 0, nearness, 0.0)
    max_sim = jnp.full((rows_local,), -1.0, F32).at[target].max(returned.reshape(-1), mode="drop")
    return (max_sim, centroid_cos)


def iota(shape, axis):
    return lax.broadcasted_iota(jnp.int32, shape, axis)


def down(values):
    return jnp.sum(values, axis=0, keepdims=True)


def across(values):
    return jnp.sum(values, axis=1, keepdims=True)


def pick(mask, values):
    return jnp.where(mask, values, 0.0)


def as_column(row):
    size = row.shape[1]
    return across(pick(iota((size, size), 0) == iota((size, size), 1), row))


def as_row(column):
    size = column.shape[0]
    return down(pick(iota((size, size), 0) == iota((size, size), 1), column))


def dot(a, b):
    return jnp.dot(a, b, preferred_element_type=F32)


def dot_rows(a, b):
    return lax.dot_general(a, b, (((1,), (1,)), ((), ())), preferred_element_type=F32)


def onehot(mask):
    return jnp.where(mask, 1.0, 0.0).astype(BF16)


def halves(values):
    first = values.astype(BF16).astype(F32)
    return first, (values - first).astype(BF16).astype(F32)


def rank_groups(count_ref):
    count_row = count_ref[...].astype(F32)
    count_column = as_column(count_row)
    sub, lane = iota((GROUPS, 128), 0), iota((GROUPS, 128), 1)
    count_lanes = down(pick(sub == lane, count_column))
    ahead = (count_column > count_lanes) | ((count_column == count_lanes) & (sub < lane))
    rank = down(jnp.where(ahead, 1.0, 0.0))
    return jnp.where(iota((1, 128), 1) < GROUPS, rank, 0.0), count_column


def place_documents(assign_ref, owner_ref, rank, earlier_ref, chip_step):
    member = iota((CLUSTERS, ROWS), 0) == assign_ref[...]
    member_low = onehot(member)
    before = down(pick(member, dot(member_low, earlier_ref[...])))
    count_column = across(jnp.where(member, 1.0, 0.0))
    owner_row = owner_ref[...].astype(F32)
    owner_column = as_column(owner_row)
    sub, lane = iota((CLUSTERS, CLUSTERS), 0), iota((CLUSTERS, CLUSTERS), 1)
    within = across(jnp.where((owner_column == owner_row) & (lane < sub), 1.0, 0.0))
    group_rank = across(pick(owner_column == lane.astype(F32), rank))
    place = group_rank * (CLUSTERS // GROUPS) + within
    chip = jnp.minimum(place, (CLUSTERS - 1) - place)
    count_row, place_row, chip_row = as_row(count_column), as_row(place), as_row(chip)
    opposite = down(pick((CLUSTERS - 1) - place == place_row, count_column))
    offset = jnp.where(place_row >= CHIPS, opposite, 0.0)
    step_row = down(pick(sub.astype(F32) == chip_row, as_column(chip_step)))
    row = iota((16, CLUSTERS), 0)
    told = pick(row == 0, owner_row) + pick(row == 1, chip_row) + pick(row == 2, step_row) + pick(row == 3, offset)
    told = dot(told.astype(BF16), member_low)
    place_counts = down(pick(place == lane.astype(F32), count_column))
    whole = told[1:4].astype(jnp.int32)
    return told[0:1], whole[0:1], whole[1:2], before.astype(jnp.int32) + whole[2:3], place_counts


def missing_documents(index_ref, count_column, group):
    listed = index_ref[...]
    live = iota((GROUPS, CAP), 1).astype(F32) < count_column
    eye = onehot(iota((CAP, CAP), 0) == iota((CAP, CAP), 1))
    high = dot_rows(eye, jnp.where(live, listed >> 4, 0).astype(F32).astype(BF16))
    low = dot_rows(eye, jnp.where(live, listed & 15, 0).astype(F32).astype(BF16))
    alive = dot_rows(eye, onehot(live))
    slots = jnp.where(alive > 0.5, high * 16.0 + low, -1.0)
    document = iota((1, ROWS), 1).astype(F32)
    lane = iota((CAP, GROUPS), 1)

    def count(g, hits):
        column = across(pick(lane == g, slots))
        wanted = jnp.where(group == g.astype(F32), document, -2.0)
        return hits + jnp.where(column == wanted, 1.0, 0.0)

    hits = lax.fori_loop(0, GROUPS, count, jnp.zeros((CAP, ROWS), F32))
    return across(jnp.where(down(hits) > 0.5, 0.0, 1.0))


def send_order():
    order = []
    for step in range(CHIPS):
        high, middle, low = step // 16, (step // 4) % 4, step % 4
        order.append((low, (middle + low) % 4, (high + middle + low) % 4))
    near = [shift for shift in order if sum(min(d, 4 - d) for d in shift) <= 1] + [(2, 0, 0)]
    near.sort(key=lambda shift: -sum(min(d, 4 - d) for d in shift))
    return [shift for shift in order if shift not in near] + near


ORDER = send_order()
SELF = CHIPS - 1


def step_to(dx, dy, dz):
    shift = (dx & 3) * 16 + (dy & 3) * 4 + (dz & 3)
    step = jnp.full(shift.shape, SELF, jnp.int32)
    for number, (x, y, z) in enumerate(ORDER[:SELF]):
        step = jnp.where(shift == x * 16 + y * 4 + z, number, step)
    return step


def in_part(step, part):
    begin, steps, _ = PARTS[part]
    return (step >= begin) & (step < begin + steps)


def chip_places():
    sub, lane = iota((CLUSTERS, CLUSTERS), 0), iota((CLUSTERS, CLUSTERS), 1)
    return onehot((sub == lane) | (sub == (CLUSTERS - 1) - lane))


def excess(totals):
    lane = iota(totals.shape, 1)
    return jnp.where(lane < CHIPS, jnp.maximum(totals - BASE, 0.0), 0.0)


def receive_plan(counts, ranks, rank, my_x, my_y, my_z, routes_ref):
    chip = my_x * 16 + my_y * 4 + my_z
    differ = jnp.where(ranks != rank, 1.0, 0.0)
    fault = across(down(differ))
    both = dot(counts.astype(BF16), chip_places())
    over = excess(both)
    lanes = iota((CHIPS, CLUSTERS), 1)
    sender = iota((CHIPS, 1), 0)
    source, target = iota((CHIPS, CHIPS), 0), iota((CHIPS, CHIPS), 1)

    same_line = (source >> 2) == (target >> 2)
    fault = fault + down(jnp.where(across(over) > BASE, 1.0, 0.0))
    of_line = dot(onehot(same_line), over.astype(BF16))
    fault = fault + across(down(jnp.where(of_line > POOL, 1.0, 0.0)))
    number = across(pick(lanes == chip, over))
    start = across(pick(same_line & (target < source), as_row(number)))

    route = routes_ref[...]
    based = jnp.where(lanes < CHIPS, jnp.minimum(both, float(BASE)), 0.0)
    for part, (_, _, room) in enumerate(PARTS):
        held = down(pick(in_part(route, part), based))
        if part == LAST:
            held = held + down(over)
        fault = fault + across(jnp.where(held > room, 1.0, 0.0))

    first = across(pick(lanes == chip, counts))
    second = across(pick(lanes == (CLUSTERS - 1) - chip, counts))
    place = (lanes & (POOL - 1)).astype(F32) - start
    mine = ((sender >> 2) == (lanes >> 3)) & (place >= 0.0) & (place < number)
    over_first = down(jnp.where(mine & (place + BASE < first), 1.0, 0.0))
    over_second = down(jnp.where(mine & (place + BASE >= first), 1.0, 0.0))
    over_first_total, over_second_total = across(over_first), across(over_second)
    earlier = onehot(iota((CLUSTERS, CLUSTERS), 0) < iota((CLUSTERS, CLUSTERS), 1))
    sub = iota((16, CLUSTERS), 0)
    before = dot((pick(sub == 0, over_first) + pick(sub == 1, over_second)).astype(BF16), earlier)

    base_first = jnp.minimum(first, float(BASE))
    base_second = jnp.minimum(first + second, float(BASE)) - base_first
    first_row, second_row = as_row(base_first), as_row(base_second)

    step_column = across(jnp.where(lanes == chip, route.astype(F32), 0.0)).astype(jnp.int32)
    step_row = as_row(step_column.astype(F32)).astype(jnp.int32)
    plans = []
    ends = []
    for part, (begin, steps, _) in enumerate(PARTS):
        inside = in_part(step_column, part)
        ahead = (target < source) & in_part(step_row, part)
        first_total = down(pick(inside, base_first))
        second_total = down(pick(inside, base_second))
        last = part == LAST
        first_end = first_total + over_first_total if last else first_total
        first_start = across(pick(ahead, first_row))
        second_start = across(pick(ahead, second_row)) + first_end
        spread = step_column - begin == (iota((CHIPS, steps * BASE), 1) >> 4)
        head, tail, head_start, tail_start = [
            down(pick(spread, column)) for column in (base_first, base_second, first_start, second_start)
        ]
        slot = (iota((1, steps * BASE), 1) & (BASE - 1)).astype(F32)
        later = jnp.where(slot < head + tail, tail_start + (slot - head), -1.0)
        plan = jnp.where(slot < head, head_start + slot, later)
        held_end = first_end + second_total
        if last:
            over_row_of = jnp.where(over_second > 0.5, held_end + before[1:2], -1.0)
            over_row_of = jnp.where(over_first > 0.5, first_total + before[0:1], over_row_of)
            plan = jnp.concatenate([plan[:, : steps * BASE - CLUSTERS], over_row_of], axis=1)
            held_end = held_end + over_second_total
        plans.append(plan)
        ends.append((first_end, held_end))
    return plans, ends, fault


def kernel(
    x_hbm, assign_hbm, owner_hbm, count_hbm, index_hbm,
    out_ref, fault_ref,
    x_ref, assign_ref, owner_ref, count_ref, index_ref,
    send, got, own_over, line_over, send_over, got_over, pick_0, pick_1,
    earlier_ref, routes_ref, way_ref, keys, facts, sums, their_sums, back, returned,
    load_sem, send_sem, recv_sem,
):
    grp, blk = lax.axis_index("grp"), lax.axis_index("blk")
    my_x, my_y, my_z, core = grp // 4, grp % 4, blk // 2, blk % 2
    my_chip = grp * 4 + my_z
    picks = (pick_0, pick_1)
    along_x = [((my_x + d) % 4) * 4 for d in range(4)]
    along_y = [(my_y + d) % 4 for d in range(4)]
    along_z = [((my_z + d) % 4) * 2 + core for d in range(4)]
    other_core = {"grp": grp, "blk": my_z * 2 + (1 - core)}

    def device_at(step, sign):
        dx, dy, dz = [(sign * d) % 4 for d in ORDER[step]]
        return {"grp": along_x[dx] + along_y[dy], "blk": along_z[dz]}

    def remote(source, target, number, device):
        return pltpu.make_async_remote_copy(
            src_ref=source,
            dst_ref=target,
            send_sem=send_sem.at[number],
            recv_sem=recv_sem.at[number],
            device_id=device,
            device_id_type=pl.DeviceIdType.MESH,
        )

    def await_blocks(ref, number, semaphore):
        block = ref.at[pl.ds(0, number)]
        pltpu.make_async_copy(block, block, semaphore).wait()

    LINE, OVER, FACTS, SUMS, BACK, SWAP, PART = 0, 1, 2, 3, 4, 5, 7
    messages = [min(begin + steps, SELF) - begin for begin, steps, _ in PARTS]

    loads = [
        pltpu.make_async_copy(source, target, load_sem.at[number])
        for number, (source, target) in enumerate(
            (
                (assign_hbm, assign_ref),
                (owner_hbm, owner_ref),
                (count_hbm, count_ref),
                (index_hbm, index_ref),
                (x_hbm, x_ref),
            )
        )
    ]
    for load in loads:
        load.start()
    barrier = pltpu.get_barrier_semaphore()
    for device in [device_at(step, 1) for step in range(SELF)] + [other_core]:
        pl.semaphore_signal(barrier, inc=1, device_id=device, device_id_type=pl.DeviceIdType.MESH)
    lane = iota((1, CLUSTERS), 1)
    chip_step = step_to((lane >> 4) - my_x, ((lane >> 2) & 3) - my_y, (lane & 3) - my_z).astype(F32)
    earlier_ref[...] = onehot(iota((ROWS, ROWS), 0) < iota((ROWS, ROWS), 1))
    for load in loads[:-1]:
        load.wait()

    rank, count_column = rank_groups(count_ref)
    group, chip, step_of, slot, place_counts = place_documents(assign_ref, owner_ref, rank, earlier_ref, chip_step)
    in_base = slot < BASE
    send_slot = jnp.where(in_base, step_of * BASE + slot, -1)
    loads[-1].wait()

    def pack(first, stop):
        slots = iota(((stop - first) * BASE, ROWS), 0) + first * BASE
        rows = dot(onehot(slots == send_slot), x_ref[...]).astype(BF16)
        send[pl.ds(first, stop - first)] = rows.reshape(stop - first, BASE, WIDTH)

    def post(first, stop):
        for step in range(first, min(stop, SELF)):
            number = max(part for part in range(len(PARTS)) if PARTS[part][0] <= step)
            remote(send.at[step], got.at[step], PART + number, device_at(step, 1)).start()

    place_counts_16 = place_counts + jnp.zeros((16, CLUSTERS), F32)
    own_excess = excess(dot(place_counts_16.astype(BF16), chip_places())[0:1])
    eye = iota((CHIPS, CLUSTERS), 0) == iota((CHIPS, CLUSTERS), 1)
    excess_column = across(pick(eye, own_excess))
    over_slot = down(pick(iota((CHIPS, ROWS), 0) < chip, excess_column)).astype(jnp.int32) + (slot - BASE)
    over_slot = jnp.where(in_base, -1, over_slot)
    row = iota((BASE, CLUSTERS), 0)
    own_over[:, :WIDTH] = dot(onehot(iota((BASE, ROWS), 0) == over_slot), x_ref[...]).astype(BF16)
    own_over[:, WIDTH:] = (pick(row == 0, place_counts) + pick(row == 1, rank)).astype(BF16)
    line_over[my_z] = own_over[...]
    sublane = iota((LINES * 2 * POOL, 1), 0)
    way = sublane >> 4
    to_chip = ((my_x + (way >> 2)) & 3) * 16 + ((my_y + way) & 3) * 4 + my_z
    way_ref[...] = onehot(iota((LINES * 2 * POOL, CLUSTERS), 1) == to_chip)
    pack(0, 8)
    pl.semaphore_wait(barrier, CHIPS)
    for d in range(1, DEPTH):
        remote(own_over, line_over.at[my_z], LINE, {"grp": grp, "blk": along_z[d]}).start()
    post(0, 8)
    pack(8, 24)
    post(8, 24)
    pack(24, 48)
    to_chip, sender = iota((CHIPS, CLUSTERS), 1), iota((CHIPS, CLUSTERS), 0)
    routes_ref[...] = step_to(
        (to_chip >> 4) - (sender >> 4), ((to_chip >> 2) & 3) - ((sender >> 2) & 3), (to_chip & 3) - (sender & 3)
    )

    await_blocks(line_over, DEPTH - 1, recv_sem.at[LINE])
    line_counts = [line_over[d, 0:1, WIDTH:].astype(F32) for d in range(DEPTH)]
    line_ranks = [line_over[d, 1:2, WIDTH:].astype(F32) for d in range(DEPTH)]
    row = iota((2 * POOL, CLUSTERS), 0)
    told = jnp.zeros((2 * POOL, CLUSTERS), F32)
    for d in range(DEPTH):
        told = told + pick(row == d, line_counts[d]) + pick(row == DEPTH + d, line_ranks[d])
    told = told.astype(BF16)
    over = excess(dot(told, chip_places()))[0:DEPTH]
    ahead = dot(over.astype(BF16), onehot(iota((CLUSTERS, CLUSTERS), 0) < iota((CLUSTERS, CLUSTERS), 1)))
    before = [jnp.zeros((1, CLUSTERS), F32)]
    for d in range(DEPTH - 1):
        before.append(before[-1] + over[d : d + 1])
    before = jnp.concatenate(before, axis=0)
    before_mine = down(pick(iota((DEPTH, 1), 0) == my_z, before))
    known = jnp.concatenate([over, ahead, before, jnp.zeros((DEPTH, CLUSTERS), F32)], axis=0).astype(BF16)
    known = dot_rows(way_ref[...], known)
    entry = iota((LINES * 2 * POOL, DEPTH * BASE), 1)

    def of_depth(kind):
        values = known[:, kind * DEPTH : kind * DEPTH + 1]
        for d in range(1, DEPTH):
            values = jnp.where((entry >> 4) == d, known[:, kind * DEPTH + d : kind * DEPTH + d + 1], values)
        return values

    offset = (entry & (BASE - 1)).astype(F32) - of_depth(1)
    position = jnp.where((offset >= 0.0) & (offset < of_depth(0)), offset + of_depth(2), -1.0)
    wanted = (sublane & (2 * POOL - 1)).astype(F32)
    blocks = line_over[:, :, :WIDTH].reshape(DEPTH * BASE, WIDTH)
    left = dot(onehot((wanted == position) & (wanted < POOL)), blocks[:, :HALF])
    right = dot(onehot((wanted - POOL == position) & (wanted >= POOL)), blocks[:, HALF:])
    send_over[:, :, :HALF] = (left + right).astype(BF16).reshape(LINES, 2 * POOL, HALF)
    for d in range(LINES):
        send_over[d, :, HALF:] = told
    got_over[grp] = send_over[0]
    for d in range(1, LINES):
        device = {"grp": along_x[d // 4] + along_y[d % 4], "blk": blk}
        remote(send_over.at[d], got_over.at[grp], OVER, device).start()
    post(24, 48)
    pack(48, CHIPS)
    post(48, CHIPS)
    got[SELF] = send[SELF]
    missing = missing_documents(index_ref, count_column, group)

    await_blocks(got_over, LINES - 1, recv_sem.at[OVER])
    told = got_over[:, :, HALF:].astype(F32)
    counts = told[:, 0:DEPTH].reshape(CHIPS, CLUSTERS)
    ranks = told[:, DEPTH : 2 * DEPTH].reshape(CHIPS, CLUSTERS)
    plans, ends, fault = receive_plan(counts, ranks, rank, my_x, my_y, my_z, routes_ref)

    row = iota((8, 128), 0)
    told = pick(row == 6, rank) + pick(row == 7, jnp.where(iota((1, 128), 1) == 0, fault, missing))
    for part, (first_end, held_end) in enumerate(ends):
        told = told + pick(row == part, first_end) + pick(row == 2 + part, held_end)
        picks[part][...] = onehot(iota(picks[part].shape, 0).astype(F32) == plans[part])
    facts[0] = told
    swap_facts = remote(facts.at[0], facts.at[1], FACTS, other_core)
    swap_facts.start()

    best = [jnp.full((1, room), -1.0, F32) for _, _, room in PARTS]
    key_kinds = []
    query_kinds = []
    totals = [jnp.zeros((1, WIDTH), F32), jnp.zeros((1, WIDTH), F32)]
    swaps = []

    def add_kinds(first, held, room):
        number = iota((room, 1), 0).astype(F32)
        key_kinds.append(jnp.where(number < first, 0.0, jnp.where(number < held, 1.0, 2.0)))

    for (first_end, held_end), (_, _, room) in zip(ends, PARTS):
        add_kinds(first_end, held_end, room)
        query_kinds.append(jnp.where(iota((1, room), 1).astype(F32) < first_end, 0.0, 1.0))

    def compare(first_key, last_key, part, more=0):
        borders = (*STARTS, *(HELD + start for start in STARTS), 2 * HELD)
        begin, stop = borders[first_key], borders[last_key + 1]
        start, room = STARTS[part], PARTS[part][2]
        scores = dot_rows(keys[begin : stop + more], keys[start : start + room])
        rest, scores = scores[stop - begin :], scores[: stop - begin]
        kind = jnp.concatenate(key_kinds[first_key : last_key + 1], axis=0)
        matched = kind == query_kinds[part]
        if begin < start + room and start < stop:
            matched = matched & (iota(kind.shape, 0) + (begin - start) != iota((1, room), 1))
        best[part] = jnp.maximum(best[part], jnp.max(jnp.where(matched, scores, -1.0), axis=0, keepdims=True))
        return rest

    def arrive(part):
        begin, steps, room = PARTS[part]
        await_blocks(got, messages[part], recv_sem.at[PART + part])
        rows = dot(picks[part][...], got[pl.ds(begin, steps)].reshape(steps * BASE, WIDTH))
        unit = rows * lax.rsqrt(across(rows * rows) + EPSILON)
        keys[pl.ds(STARTS[part], room)] = unit.astype(BF16)
        swap = remote(
            keys.at[pl.ds(STARTS[part], room)], keys.at[pl.ds(HELD + STARTS[part], room)], SWAP + part, other_core
        )
        swap.start()
        swaps.append(swap)
        is_first = iota((room, 1), 0).astype(F32) < ends[part][0]
        totals[0] = totals[0] + down(pick(is_first, unit))
        totals[1] = totals[1] + down(jnp.where(is_first, 0.0, unit))

    arrive(0)
    compare(0, 0, 0)
    swap_facts.wait()
    their_told = facts[1]
    for part, (_, _, room) in enumerate(PARTS):
        add_kinds(their_told[part : part + 1, 0:1], their_told[2 + part : 3 + part, 0:1], room)
    half_rows = got_over[:, :, :HALF].reshape(LINES * 2 * POOL, HALF)
    shape = (LINES * POOL, LINES * 2 * POOL)
    to, at = iota(shape, 0), iota(shape, 1)
    same = ((to >> 3) == (at >> 4)) & ((to & 7) == (at & 7))
    left = dot(onehot(same & ((at & POOL) == 0)), half_rows)
    right = dot(onehot(same & ((at & POOL) != 0)), half_rows)
    whole = jnp.concatenate([left, right], axis=1).astype(BF16)
    got[pl.ds(CHIPS, TOTAL - CHIPS)] = whole.reshape(TOTAL - CHIPS, BASE, WIDTH)
    swaps[0].wait()
    compare(2, 2, 0)

    arrive(1)
    row = iota((8, WIDTH), 0)
    sums[...] = pick(row == 0, totals[0]) + pick(row == 1, totals[1])
    swap_sums = remote(sums, their_sums, SUMS, other_core)
    swap_sums.start()
    compare(0, 2, 1)
    compare(1, 1, 0)

    swap_sums.wait()
    total = sums[...] + their_sums[...]
    keys[pl.ds(2 * HELD, 16)] = jnp.concatenate(halves(total), axis=0).astype(BF16)
    scale = lax.rsqrt(across(total * total) + EPSILON)
    swaps[1].wait()
    near = [compare(3, 3, part, 16) for part in range(len(PARTS))]
    near = [(some[0:8] + some[8:16]) * scale for some in near]

    poison = missing + their_told[7:8, 1:2] > 0.5
    tiles = CHIPS * BASE // 128
    for part, (begin, steps, room) in enumerate(PARTS):
        row = iota((8, room), 0)
        query_number = iota((1, room), 1).astype(F32)
        some = jnp.where(query_number < ends[part][0], near[part][0:1], near[part][1:2])
        values = jnp.zeros((8, room), F32)
        for number, term in enumerate(halves(best[part]) + halves(some)):
            values = jnp.where(row == number, term, values)
        out = dot(values.astype(BF16), picks[part][...])
        for kind in range(2):
            line = out[2 * kind : 2 * kind + 1] + out[2 * kind + 1 : 2 * kind + 2]
            line = jnp.where(poison, NONE, line)
            for tile in range(steps * BASE // 128):
                piece = line[:, tile * 128 : (tile + 1) * 128]
                to = begin * BASE // 128 + tile
                if to < tiles:
                    back[to, kind : kind + 1, :] = piece
                else:
                    for each in range(tiles):
                        back[each, 2 + kind : 3 + kind, :] = piece
    returned[SELF] = back[SELF // 8]
    for step in range(SELF):
        remote(back.at[step // 8], returned.at[step], BACK, device_at(step, -1)).start()

    differ = across(jnp.where(their_told[6:7] != rank, 1.0, 0.0))
    fault = fault + their_told[7:8, 0:1] + differ
    chosen = onehot(iota((CHIPS, ROWS), 0) == step_of)
    sub = iota((128, ROWS), 0)
    at_base = (sub == (step_of & 7) * BASE + slot) & in_base
    before_column = across(pick(eye, before_mine))
    line_slot = down(pick(iota((CHIPS, ROWS), 0) == chip, before_column)).astype(jnp.int32)
    at_over = (sub == grp * POOL + line_slot + (slot - BASE)) & (~in_base)

    await_blocks(returned, CHIPS - 1, recv_sem.at[BACK])
    found = []
    for number in range(4):
        line = returned[:, number, :]
        if number == 0:
            poisoned = across(down(jnp.where(line > 0.5 * NONE, 1.0, 0.0)))
            fault_ref[...] = jnp.where(fault + poisoned > 0.5, 1, 0) + jnp.zeros((1, 128), jnp.int32)
        terms = jnp.concatenate(halves(line), axis=1).astype(BF16)
        out = lax.dot_general(terms, chosen, (((0,), (0,)), ((), ())), preferred_element_type=F32)
        found.append(out[0:128] + out[128:256])
    out_ref[0:1] = down(pick(at_base, found[0]) + pick(at_over, found[2]))
    out_ref[1:2] = down(pick(at_base, found[1]) + pick(at_over, found[3]))

    await_blocks(line_over, DEPTH - 1, send_sem.at[LINE])
    await_blocks(got_over, LINES - 1, send_sem.at[OVER])
    await_blocks(returned, CHIPS - 1, send_sem.at[BACK])
    for part in range(len(PARTS)):
        await_blocks(got, messages[part], send_sem.at[PART + part])


def routed(embeddings, assign, owner, send_count, send_index):
    return pl.pallas_call(
        kernel,
        out_shape=(
            jax.ShapeDtypeStruct((2, ROWS), F32),
            jax.ShapeDtypeStruct((1, 128), jnp.int32),
        ),
        in_specs=[pl.BlockSpec(memory_space=pl.ANY)] * 5,
        out_specs=(pl.BlockSpec(memory_space=pltpu.VMEM),) * 2,
        scratch_shapes=[
            pltpu.VMEM((ROWS, WIDTH), BF16),
            pltpu.VMEM((1, ROWS), jnp.int32),
            pltpu.VMEM((1, CLUSTERS), jnp.int32),
            pltpu.VMEM((1, GROUPS), jnp.int32),
            pltpu.VMEM((GROUPS, CAP), jnp.int32),
            pltpu.VMEM((CHIPS, BASE, WIDTH), BF16),
            pltpu.VMEM((TOTAL, BASE, WIDTH), BF16),
            pltpu.VMEM((BASE, WIDTH + CLUSTERS), BF16),
            pltpu.VMEM((DEPTH, BASE, WIDTH + CLUSTERS), BF16),
            pltpu.VMEM((LINES, 2 * POOL, HALF + CLUSTERS), BF16),
            pltpu.VMEM((LINES, 2 * POOL, HALF + CLUSTERS), BF16),
            *[pltpu.VMEM((room, steps * BASE), BF16) for _, steps, room in PARTS],
            pltpu.VMEM((ROWS, ROWS), BF16),
            pltpu.VMEM((CHIPS, CLUSTERS), jnp.int32),
            pltpu.VMEM((LINES * 2 * POOL, CLUSTERS), BF16),
            pltpu.VMEM((2 * HELD + 16, WIDTH), BF16),
            pltpu.VMEM((2, 8, 128), F32),
            pltpu.VMEM((8, WIDTH), F32),
            pltpu.VMEM((8, WIDTH), F32),
            pltpu.VMEM((CHIPS * BASE // 128, 4, 128), F32),
            pltpu.VMEM((CHIPS, 4, 128), F32),
            pltpu.SemaphoreType.DMA((5,)),
            pltpu.SemaphoreType.DMA((9,)),
            pltpu.SemaphoreType.DMA((9,)),
        ],
        compiler_params=pltpu.CompilerParams(
            collective_id=0, has_side_effects=True, vmem_limit_bytes=48 * 1024 * 1024
        ),
    )(
        embeddings,
        assign.reshape(1, ROWS),
        owner.reshape(1, CLUSTERS),
        send_count,
        send_index[0],
    )


def body(embeddings, assign, owner, send_count, send_index):
    arguments = (embeddings, assign, owner, send_count, send_index)
    results, fault = routed(*arguments)
    results = lax.cond(fault[0, 0] != 0, lambda: jnp.stack(general(*arguments)), lambda: results)
    return results[0], results[1]


def solution(mesh):
    placed = (
        P(("grp", "blk"), None),
        P(("grp", "blk")),
        P(),
        P(("grp", "blk"), None),
        P(("grp", "blk"), None, None),
    )
    return jax.shard_map(
        body,
        mesh=mesh,
        in_specs=placed,
        out_specs=(P(("grp", "blk")), P(("grp", "blk"))),
        check_vma=False,
    )
```

profile of v0, /device:TPU:1, one launch (start us, length us, event | category | flops | bytes accessed | tf_op | source)
XLA Modules:
  0.0 62.0 jit_solution(11727692179889007675)
XLA Ops:
  7.2 47.2 %shard_map.68 = (f32[2,512]{1,0:T(2,128)S(1)}, s32[1,128]{1,0:T(1,128)S(1)}) custom-call(bf16[512,768]{1,0:T(8,128)(2,1)} %x_hbm.1, s32[1,512]{1,0:T(1,128)} %bitcast.51, s32[1,128]{1,0:T(1,128)} %bitcast.50, s32[1,16]{1,0:T(1,128)} %count_hbm.1, s32[16,64]{1,0:T(8,128)} %bitcast.55), custom_call_target="tpu_custom_call" | custom-call | tf_op jit(solution)/shard_map/pallas_call | solution.py:605
  54.4 0.2 conditional.1
  54.6 0.6 fusion.16
where the time goes:
time: 62.2 us; the launch traced here: 62 us
  Pallas kernels  47.2 us (76%)
  between operations  14.1 us (23%)
    pallas_call x1, Pallas kernels, routed(): pl.pallas_call(kernel, out_shape=(jax.ShapeDtypeStruct((2, ROWS), F32), j...  47.2 us

commit v1 on v0

--- a/solution.py
+++ b/solution.py
@@ -240,8 +240,6 @@
 
 def receive_plan(counts, ranks, rank, my_x, my_y, my_z, routes_ref):
     chip = my_x * 16 + my_y * 4 + my_z
-    differ = jnp.where(ranks != rank, 1.0, 0.0)
-    fault = across(down(differ))
     both = dot(counts.astype(BF16), chip_places())
     over = excess(both)
     lanes = iota((CHIPS, CLUSTERS), 1)
@@ -249,19 +247,20 @@
     source, target = iota((CHIPS, CHIPS), 0), iota((CHIPS, CHIPS), 1)
 
     same_line = (source >> 2) == (target >> 2)
-    fault = fault + down(jnp.where(across(over) > BASE, 1.0, 0.0))
-    of_line = dot(onehot(same_line), over.astype(BF16))
-    fault = fault + across(down(jnp.where(of_line > POOL, 1.0, 0.0)))
     number = across(pick(lanes == chip, over))
     start = across(pick(same_line & (target < source), as_row(number)))
 
-    route = routes_ref[...]
-    based = jnp.where(lanes < CHIPS, jnp.minimum(both, float(BASE)), 0.0)
-    for part, (_, _, room) in enumerate(PARTS):
-        held = down(pick(in_part(route, part), based))
-        if part == LAST:
-            held = held + down(over)
-        fault = fault + across(jnp.where(held > room, 1.0, 0.0))
+    def faults():
+        differ = jnp.where(ranks != rank, 1.0, 0.0)
+        differ = differ + jnp.where(dot(onehot(same_line), over.astype(BF16)) > POOL, 1.0, 0.0)
+        based = jnp.where(lanes < CHIPS, jnp.minimum(both, float(BASE)), 0.0)
+        fault = across(down(differ)) + down(jnp.where(across(over) > BASE, 1.0, 0.0))
+        for part, (_, _, room) in enumerate(PARTS):
+            held = down(pick(in_part(routes_ref[...], part), based))
+            if part == LAST:
+                held = held + down(over)
+            fault = fault + across(jnp.where(held > room, 1.0, 0.0))
+        return fault
 
     first = across(pick(lanes == chip, counts))
     second = across(pick(lanes == (CLUSTERS - 1) - chip, counts))
@@ -278,7 +277,7 @@
     base_second = jnp.minimum(first + second, float(BASE)) - base_first
     first_row, second_row = as_row(base_first), as_row(base_second)
 
-    step_column = across(jnp.where(lanes == chip, route.astype(F32), 0.0)).astype(jnp.int32)
+    step_column = across(jnp.where(lanes == chip, routes_ref[...].astype(F32), 0.0)).astype(jnp.int32)
     step_row = as_row(step_column.astype(F32)).astype(jnp.int32)
     plans = []
     ends = []
@@ -306,7 +305,7 @@
             held_end = held_end + over_second_total
         plans.append(plan)
         ends.append((first_end, held_end))
-    return plans, ends, fault
+    return plans, ends, faults
 
 
 def kernel(
@@ -400,18 +399,11 @@
     way = sublane >> 4
     to_chip = ((my_x + (way >> 2)) & 3) * 16 + ((my_y + way) & 3) * 4 + my_z
     way_ref[...] = onehot(iota((LINES * 2 * POOL, CLUSTERS), 1) == to_chip)
-    pack(0, 8)
+    pack(0, 16)
     pl.semaphore_wait(barrier, CHIPS)
     for d in range(1, DEPTH):
         remote(own_over, line_over.at[my_z], LINE, {"grp": grp, "blk": along_z[d]}).start()
-    post(0, 8)
-    pack(8, 24)
-    post(8, 24)
-    pack(24, 48)
-    to_chip, sender = iota((CHIPS, CLUSTERS), 1), iota((CHIPS, CLUSTERS), 0)
-    routes_ref[...] = step_to(
-        (to_chip >> 4) - (sender >> 4), ((to_chip >> 2) & 3) - ((sender >> 2) & 3), (to_chip & 3) - (sender & 3)
-    )
+    post(0, 16)
 
     await_blocks(line_over, DEPTH - 1, recv_sem.at[LINE])
     line_counts = [line_over[d, 0:1, WIDTH:].astype(F32) for d in range(DEPTH)]
@@ -451,20 +443,25 @@
     for d in range(1, LINES):
         device = {"grp": along_x[d // 4] + along_y[d % 4], "blk": blk}
         remote(send_over.at[d], got_over.at[grp], OVER, device).start()
-    post(24, 48)
-    pack(48, CHIPS)
-    post(48, CHIPS)
+    pack(16, 40)
+    post(16, 40)
+    pack(40, CHIPS)
+    post(40, CHIPS)
     got[SELF] = send[SELF]
+    to_chip, sender = iota((CHIPS, CLUSTERS), 1), iota((CHIPS, CLUSTERS), 0)
+    routes_ref[...] = step_to(
+        (to_chip >> 4) - (sender >> 4), ((to_chip >> 2) & 3) - ((sender >> 2) & 3), (to_chip & 3) - (sender & 3)
+    )
     missing = missing_documents(index_ref, count_column, group)
 
     await_blocks(got_over, LINES - 1, recv_sem.at[OVER])
     told = got_over[:, :, HALF:].astype(F32)
     counts = told[:, 0:DEPTH].reshape(CHIPS, CLUSTERS)
     ranks = told[:, DEPTH : 2 * DEPTH].reshape(CHIPS, CLUSTERS)
-    plans, ends, fault = receive_plan(counts, ranks, rank, my_x, my_y, my_z, routes_ref)
+    plans, ends, faults = receive_plan(counts, ranks, rank, my_x, my_y, my_z, routes_ref)
 
     row = iota((8, 128), 0)
-    told = pick(row == 6, rank) + pick(row == 7, jnp.where(iota((1, 128), 1) == 0, fault, missing))
+    told = pick(row == 6, rank) + pick(row == 7, missing)
     for part, (first_end, held_end) in enumerate(ends):
         told = told + pick(row == part, first_end) + pick(row == 2 + part, held_end)
         picks[part][...] = onehot(iota(picks[part].shape, 0).astype(F32) == plans[part])
@@ -515,6 +512,7 @@
         totals[1] = totals[1] + down(jnp.where(is_first, 0.0, unit))
 
     arrive(0)
+    fault = faults()
     compare(0, 0, 0)
     swap_facts.wait()
     their_told = facts[1]
@@ -533,14 +531,14 @@
 
     arrive(1)
     row = iota((8, WIDTH), 0)
-    sums[...] = pick(row == 0, totals[0]) + pick(row == 1, totals[1])
+    sums[...] = pick(row == 0, totals[0]) + pick(row == 1, totals[1]) + pick(row == 2, fault)
     swap_sums = remote(sums, their_sums, SUMS, other_core)
     swap_sums.start()
     compare(0, 2, 1)
     compare(1, 1, 0)
 
     swap_sums.wait()
-    total = sums[...] + their_sums[...]
+    total = pick(row < 2, sums[...] + their_sums[...])
     keys[pl.ds(2 * HELD, 16)] = jnp.concatenate(halves(total), axis=0).astype(BF16)
     scale = lax.rsqrt(across(total * total) + EPSILON)
     swaps[1].wait()
@@ -573,7 +571,7 @@
         remote(back.at[step // 8], returned.at[step], BACK, device_at(step, -1)).start()
 
     differ = across(jnp.where(their_told[6:7] != rank, 1.0, 0.0))
-    fault = fault + their_told[7:8, 0:1] + differ
+    fault = fault + their_sums[2:3, 0:1] + differ
     chosen = onehot(iota((CHIPS, ROWS), 0) == step_of)
     sub = iota((128, ROWS), 0)
     at_base = (sub == (step_of & 7) * BASE + slot) & in_base

time: 62.2 us -> 62.9 us (1.011)
  Pallas kernels: 47.2 us -> 47.9 us
    pallas_call x1, Pallas kernels: 47.2 us -> 47.9 us  [routed(): pl.pallas_call(kernel, out_shape=(jax.ShapeDtypeStruct((2, ROWS), F32), j...]
where the time goes in v1:
time: 62.9 us; the launch traced here: 62.8 us
  Pallas kernels  47.9 us (76%)
  between operations  14.1 us (22%)
    pallas_call x1, Pallas kernels, routed(): pl.pallas_call(kernel, out_shape=(jax.ShapeDtypeStruct((2, ROWS), F32), j...  47.9 us

profile of v1, /device:TPU:1, one launch (start us, length us, event | category | flops | bytes accessed | tf_op | source)
XLA Modules:
  0.0 62.8 jit_solution(13172680671075300832)
XLA Ops:
  7.2 47.9 %shard_map.68 = (f32[2,512]{1,0:T(2,128)S(1)}, s32[1,128]{1,0:T(1,128)S(1)}) custom-call(bf16[512,768]{1,0:T(8,128)(2,1)} %x_hbm.1, s32[1,512]{1,0:T(1,128)} %bitcast.51, s32[1,128]{1,0:T(1,128)} %bitcast.50, s32[1,16]{1,0:T(1,128)} %count_hbm.1, s32[16,64]{1,0:T(8,128)} %bitcast.55), custom_call_target="tpu_custom_call" | custom-call | tf_op jit(solution)/shard_map/pallas_call | solution.py:603
  55.1 0.2 conditional.1
  55.4 0.6 fusion.16

commit v2 on v1

--- a/solution.py
+++ b/solution.py
@@ -404,6 +404,8 @@
     for d in range(1, DEPTH):
         remote(own_over, line_over.at[my_z], LINE, {"grp": grp, "blk": along_z[d]}).start()
     post(0, 16)
+    pack(16, 24)
+    post(16, 24)
 
     await_blocks(line_over, DEPTH - 1, recv_sem.at[LINE])
     line_counts = [line_over[d, 0:1, WIDTH:].astype(F32) for d in range(DEPTH)]
@@ -443,10 +445,10 @@
     for d in range(1, LINES):
         device = {"grp": along_x[d // 4] + along_y[d % 4], "blk": blk}
         remote(send_over.at[d], got_over.at[grp], OVER, device).start()
-    pack(16, 40)
-    post(16, 40)
-    pack(40, CHIPS)
-    post(40, CHIPS)
+    pack(24, 48)
+    post(24, 48)
+    pack(48, CHIPS)
+    post(48, CHIPS)
     got[SELF] = send[SELF]
     to_chip, sender = iota((CHIPS, CLUSTERS), 1), iota((CHIPS, CLUSTERS), 0)
     routes_ref[...] = step_to(

time: 62.9 us -> 62 us (0.986)
  Pallas kernels: 47.9 us -> 47 us
    pallas_call x1, Pallas kernels: 47.9 us -> 47 us  [routed(): pl.pallas_call(kernel, out_shape=(jax.ShapeDtypeStruct((2, ROWS), F32), j...]
where the time goes in v2:
time: 62 us; the launch traced here: 61.9 us
  Pallas kernels  47 us (76%)
  between operations  14.1 us (23%)
    pallas_call x1, Pallas kernels, routed(): pl.pallas_call(kernel, out_shape=(jax.ShapeDtypeStruct((2, ROWS), F32), j...  47 us

profile of v2, /device:TPU:1, one launch (start us, length us, event | category | flops | bytes accessed | tf_op | source)
XLA Modules:
  0.0 61.9 jit_solution(17669935516497927733)
XLA Ops:
  7.2 47.0 %shard_map.68 = (f32[2,512]{1,0:T(2,128)S(1)}, s32[1,128]{1,0:T(1,128)S(1)}) custom-call(bf16[512,768]{1,0:T(8,128)(2,1)} %x_hbm.1, s32[1,512]{1,0:T(1,128)} %bitcast.51, s32[1,128]{1,0:T(1,128)} %bitcast.50, s32[1,16]{1,0:T(1,128)} %count_hbm.1, s32[16,64]{1,0:T(8,128)} %bitcast.55), custom_call_target="tpu_custom_call" | custom-call | tf_op jit(solution)/shard_map/pallas_call | solution.py:605
  54.2 0.2 conditional.1
  54.4 0.6 fusion.16
